TPU v7x, 32 devices: a whole 2x2x4 slice. The times are simulated.
32 devices in a mesh: groups: 2 (over y), space: 4 (over z), tangent: 4 (over x, core).
Axes of the slice: x: 2, y: 2, z: 4, core: 2. Of those that a mesh axis runs over, the one named last changes fastest.
Arguments:
- positions: float32 [16, 2, 128], P(('groups', 'space')), parts along dimension 0, may hold values from 0.45 to 15.55, as said below
- momenta: float32 [16, 2, 128], P(('groups', 'space')), parts along dimension 0, may hold values from -4 to 4
- cell_count: int32 [16], P(('groups', 'space')), parts along dimension 0, may hold values from 64 to 128, as said below
- tangent: float32 [16, 4, 128, 1024], P(('groups', 'space'), None, None, 'tangent'), parts along dimension 0, may hold values from -6 to 6
Outputs:
- phase: float32 [16, 4, 128], P(('groups', 'space')), parts along dimension 0
- new_tangent: float32 [16, 4, 128, 1024], P(('groups', 'space'), None, None, 'tangent'), parts along dimension 0
- stretch: float32 [2048], P(('groups', 'tangent')), parts along dimension 0
There are 2 independent parts, one for each index of `groups`. A program takes and returns all parts, laid end to end along the dimension named above; each array names one. Nothing has to cross between parts.
Inputs may be any that keep to these rules, and one draw needn't show every extreme that they name: Slots 0 to cell_count - 1 of a cell hold particles, the others are padding; some cell holds 128 particles in every draw. `positions`: every slot of a cell, padding too, lies within 0.05 in each coordinate of its own point of the lattice (m + 0.5, n + 0.5), m from 0 to 7, n from 0 to 15; no two slots of a cell share a lattice point.
All inputs are finite; a program needn't handle non-finite values.
Results may differ from a plain program's by a relative error of at most 0.006.
Values may be sent and summed in bfloat16 or wider, within the bound.
No kernel may reach another device: no remote copies, remote signals or barrier semaphores. Data moves between devices by JAX's collectives and lax.ppermute only.
A program may use at most 128 MiB of HBM per device.

v0:
```python
import jax
import jax.numpy as jnp
from jax import lax
from jax.sharding import PartitionSpec as P

STEPS = 2
DT = 0.005
CUT2 = 2.0 ** (1.0 / 3.0)
PARK = 1000.0
HIGH = lax.Precision.HIGHEST


def padded(block, sides, width):
    for axis, dim in sides:
        count = lax.axis_size(axis)
        forward = [(i, i + 1) for i in range(count - 1)]
        forward.append((count - 1, 0))
        backward = [(target, source) for source, target in forward]
        low = lax.ppermute(
            lax.slice_in_dim(block, block.shape[dim] - width, None, axis=dim), axis, forward
        )
        high = lax.ppermute(lax.slice_in_dim(block, 0, width, axis=dim), axis, backward)
        block = jnp.concatenate([low, block, high], axis=dim)
    return block


def pair_terms(own_coords, own_alive, far_coords, shift_x, shift_y, same_cell):
    delta_x = shift_x + far_coords[:, 0, None, :] - own_coords[:, 0, :, None]
    delta_y = shift_y + far_coords[:, 1, None, :] - own_coords[:, 1, :, None]
    dist2 = delta_x * delta_x + delta_y * delta_y
    within = jnp.logical_and(dist2 < CUT2, own_alive[:, :, None] > 0.5)
    if same_cell:
        within = jnp.logical_and(within, jnp.logical_not(jnp.eye(dist2.shape[-1], dtype=bool)))
    weight = within.astype(jnp.float32)
    safe = jnp.where(within, dist2, CUT2)
    inverse = 1.0 / safe
    inv_three = inverse * inverse * inverse
    inv_six = inv_three * inv_three
    energy = 4.0 * (inv_six - inv_three) + 1.0
    energy_1 = 4.0 * (3.0 * inv_three - 6.0 * inv_six) * inverse
    energy_2 = 4.0 * (42.0 * inv_six - 12.0 * inv_three) * inverse * inverse
    taper = 1.0 - safe / CUT2
    switch = taper * taper
    switch_1 = -2.0 * taper / CUT2
    switch_2 = 2.0 / (CUT2 * CUT2)
    grad_1 = (energy_1 * switch + energy * switch_1) * weight
    grad_2 = (energy_2 * switch + 2.0 * energy_1 * switch_1 + energy * switch_2) * weight
    pull_x = 2.0 * grad_1 * delta_x
    pull_y = 2.0 * grad_1 * delta_y
    k_xx = (2.0 * grad_1 + 4.0 * grad_2 * delta_x * delta_x).astype(jnp.bfloat16)
    k_xy = (4.0 * grad_2 * delta_x * delta_y).astype(jnp.bfloat16)
    k_yy = (2.0 * grad_1 + 4.0 * grad_2 * delta_y * delta_y).astype(jnp.bfloat16)
    return (pull_x, pull_y, k_xx, k_xy, k_yy)


def apply_rows(k_xx, k_xy, k_yy, far_low):
    gain_x = jnp.einsum(
        "cij,cjv->civ", k_xx, far_low[:, 0], preferred_element_type=jnp.float32
    ) + jnp.einsum("cij,cjv->civ", k_xy, far_low[:, 1], preferred_element_type=jnp.float32)
    gain_y = jnp.einsum(
        "cij,cjv->civ", k_xy, far_low[:, 0], preferred_element_type=jnp.float32
    ) + jnp.einsum("cij,cjv->civ", k_yy, far_low[:, 1], preferred_element_type=jnp.float32)
    return (gain_x, gain_y)


def add_pair(totals, parked, occupied, far_coords, far_low, shift_x, shift_y, same_cell):
    forces_x, forces_y, push_x, push_y, diag_xx, diag_xy, diag_yy = totals
    pull_x, pull_y, k_xx, k_xy, k_yy = pair_terms(
        parked, occupied, far_coords, shift_x, shift_y, same_cell
    )
    gain_x, gain_y = apply_rows(k_xx, k_xy, k_yy, far_low)
    totals = (
        forces_x + jnp.sum(pull_x, axis=2),
        forces_y + jnp.sum(pull_y, axis=2),
        push_x + gain_x,
        push_y + gain_y,
        diag_xx + jnp.sum(k_xx.astype(jnp.float32), axis=2),
        diag_xy + jnp.sum(k_xy.astype(jnp.float32), axis=2),
        diag_yy + jnp.sum(k_yy.astype(jnp.float32), axis=2),
    )
    return (totals, (pull_x, pull_y, k_xx, k_xy, k_yy))


def evaluate(coords, occupied, small_q):
    cell_total = coords.shape[0]
    low = small_q.astype(jnp.bfloat16)
    parked = jnp.concatenate(
        [coords[:, 0:1] + PARK * (1.0 - occupied)[:, None, :], coords[:, 1:2]], axis=1
    )
    empty_rows = jnp.zeros(occupied.shape, jnp.float32)
    empty_push = jnp.zeros(small_q[:, 0].shape, jnp.float32)
    totals = (empty_rows, empty_rows, empty_push, empty_push, empty_rows, empty_rows, empty_rows)
    far_low = padded(low, (("space", 0),), cell_total)
    far_coords = padded(parked, (("space", 0),), cell_total)
    for side in (-1, 0, 1):
        if side == 0:
            block_low = low
            block_coords = parked
        else:
            begin = (1 + side) * cell_total
            block_low = far_low[begin : begin + cell_total]
            block_coords = far_coords[begin : begin + cell_total]
        for lane in (-1, 0, 1):
            totals, unused = add_pair(
                totals,
                parked,
                occupied,
                jnp.roll(block_coords, -lane, axis=0),
                jnp.roll(block_low, -lane, axis=0),
                8.0 * side,
                16.0 * lane,
                side == 0 and lane == 0,
            )
    forces_x, forces_y, push_x, push_y, diag_xx, diag_xy, diag_yy = totals
    wide_own = low.astype(jnp.float32)
    push_x = push_x - diag_xx[..., None] * wide_own[:, 0] - diag_xy[..., None] * wide_own[:, 1]
    push_y = push_y - diag_xy[..., None] * wide_own[:, 0] - diag_yy[..., None] * wide_own[:, 1]
    forces = jnp.stack([forces_x, forces_y], axis=1)
    pushes = jnp.stack([push_x, push_y], axis=1)
    return (forces, pushes)


def body(positions, momenta, cell_count, tangent):
    cell_total = positions.shape[0]
    slot_count = positions.shape[2]
    block_cols = tangent.shape[3]
    occupied = (
        lax.broadcasted_iota(jnp.int32, (cell_total, slot_count), 1) < cell_count[:, None]
    ).astype(jnp.float32)
    state = tangent * occupied[:, None, :, None]
    coords = positions
    speeds = momenta
    small_q = state[:, 0:2]
    small_p = state[:, 2:4]
    forces, pushes = evaluate(coords, occupied, small_q)
    for step_index in range(STEPS):
        midway_p = speeds + 0.5 * DT * forces
        midway_dp = small_p + 0.5 * DT * pushes
        coords = coords + DT * midway_p
        small_q = small_q + DT * midway_dp
        forces, pushes = evaluate(coords, occupied, small_q)
        speeds = midway_p + 0.5 * DT * forces
        small_p = midway_dp + 0.5 * DT * pushes
    phase = jnp.concatenate([coords, speeds], axis=1)
    final = jnp.concatenate([small_q, small_p], axis=1)
    rows_form = lax.all_to_all(final, "tangent", split_axis=2, concat_axis=3, tiled=True)
    full_width = rows_form.shape[3]
    flat_rows = rows_form.reshape(-1, full_width)
    partial_value = lax.dot_general(
        flat_rows,
        flat_rows,
        (((0,), (0,)), ((), ())),
        precision=HIGH,
        preferred_element_type=jnp.float32,
    )
    gram_scale = 1.0 / (4.0 * slot_count * cell_total * lax.axis_size("space"))
    gram = lax.psum(partial_value, ("space", "tangent"))
    factor = jnp.linalg.cholesky(gram * gram_scale)
    solved = jax.scipy.linalg.solve_triangular(factor, flat_rows.T, lower=True).T
    columns_out = lax.all_to_all(
        solved.reshape(rows_form.shape), "tangent", split_axis=3, concat_axis=2, tiled=True
    )
    log_diag = jnp.log(jnp.diagonal(factor))
    stretch = lax.dynamic_slice_in_dim(log_diag, lax.axis_index("tangent") * block_cols, block_cols)
    return (phase, columns_out, stretch)


def solution(mesh):
    placed = (
        P(("groups", "space"), None, None),
        P(("groups", "space"), None, None),
        P(("groups", "space")),
        P(("groups", "space"), None, None, "tangent"),
    )
    return jax.shard_map(
        body,
        mesh=mesh,
        in_specs=placed,
        out_specs=(
            P(("groups", "space"), None, None),
            P(("groups", "space"), None, None, "tangent"),
            P(("groups", "tangent")),
        ),
        check_vma=False,
    )
```

profile of v0, /device:TPU:1, one launch (start us, length us, event | category | flops | bytes accessed | tf_op | source)
XLA Modules:
  0.0 639.7 jit_solution(17771305510368086692)
XLA Ops:
  86.5 7.0 %collective-permute-done.10 = bf16[2,2,128,256]{3,2,0,1:T(8,128)(2,1)S(1)} collective-permute-done((bf16[2,2,128,256]{3,2,0,1:T(8,128)(2,1)S(1)}, bf16[2,2,128,256]{3,2,0,1:T(8,128)(2,1)S(1)}, u32[]{:S(2)}, u32[]{:S(2)}) %collective-permute-start.10) | collective-permute-done | bytes 262176 | tf_op jit(solution)/shard_map/ppermute | solution.py:19
  105.5 21.8 %all_to_all.33 = f32[2,4,128,256]{3,0,1,2:T(2,128)S(1)} all-to-all(f32[2,4,128,256]{3,0,1,2:T(2,128)S(1)} %copy.18), channel_id=1, replica_groups=mesh['groups'=2,'space'=4,'tangent'=4] {'tangent'}, dimensions={2} | all-to-all | bytes 2097152 | tf_op jit(solution)/shard_map/all_to_all | solution.py:146
  133.8 107.8 %all-reduce.3.cloned.1.call-done = f32[1024,1024]{0,1:T(8,128)} async-done(((f32[1024,1024]{0,1:T(8,128)}), f32[1024,1024]{0,1:T(8,128)}) %all-reduce.3.cloned.1.call-update) | async-done | bytes 4194320 | tf_op jit(solution)/shard_map/psum | solution.py:157
  246.6 5.7 copy.21
  258.7 11.7 %cholesky.187 = f32[128,128]{1,0:T(8,128)S(1)} custom-call(f32[128,128]{1,0:T(8,128)S(1)} %cholesky.514), custom_call_target="Cholesky" | custom-call | tf_op jit(solution)/shard_map/jit(cholesky)/cholesky | solution.py:158
  271.1 9.8 %custom-call.63 = f32[1,128,128]{1,2,0:T(8,128)S(1)} custom-call(f32[1,128,128]{2,1,0:T(8,128)S(1)} %get-tuple-element.432), custom_call_target="InvertDiagBlocksLowerTriangular" | custom-call | tf_op jit(solution)/shard_map/jit(cholesky)/cholesky | solution.py:158
  287.3 11.9 %cholesky.209 = f32[128,128]{1,0:T(8,128)S(1)} custom-call(f32[128,128]{1,0:T(8,128)S(1)} %cholesky.518), custom_call_target="Cholesky" | custom-call | tf_op jit(solution)/shard_map/jit(cholesky)/cholesky | solution.py:158
  300.5 9.8 %custom-call.64 = f32[1,128,128]{1,2,0:T(8,128)S(1)} custom-call(f32[1,128,128]{2,1,0:T(8,128)S(1)} %get-tuple-element.429), custom_call_target="InvertDiagBlocksLowerTriangular" | custom-call | tf_op jit(solution)/shard_map/jit(cholesky)/cholesky | solution.py:158
  313.6 11.7 %cholesky.402 = f32[128,128]{1,0:T(8,128)S(1)} custom-call(f32[128,128]{1,0:T(8,128)S(1)} %cholesky.523), custom_call_target="Cholesky" | custom-call | tf_op jit(solution)/shard_map/jit(cholesky)/cholesky | solution.py:158
  326.6 9.8 %custom-call.65 = f32[1,128,128]{1,2,0:T(8,128)S(1)} custom-call(f32[1,128,128]{2,1,0:T(8,128)S(1)} %get-tuple-element.426), custom_call_target="InvertDiagBlocksLowerTriangular" | custom-call | tf_op jit(solution)/shard_map/jit(cholesky)/cholesky | solution.py:158
  340.0 11.9 %cholesky.421 = f32[128,128]{1,0:T(8,128)S(1)} custom-call(f32[128,128]{1,0:T(8,128)S(1)} %cholesky.528), custom_call_target="Cholesky" | custom-call | tf_op jit(solution)/shard_map/jit(cholesky)/cholesky | solution.py:158
  353.3 9.8 %custom-call.66 = f32[1,128,128]{1,2,0:T(8,128)S(1)} custom-call(f32[1,128,128]{2,1,0:T(8,128)S(1)} %get-tuple-element.423), custom_call_target="InvertDiagBlocksLowerTriangular" | custom-call | tf_op jit(solution)/shard_map/jit(cholesky)/cholesky | solution.py:158
  366.5 11.7 %cholesky.440 = f32[128,128]{1,0:T(8,128)S(1)} custom-call(f32[128,128]{1,0:T(8,128)S(1)} %cholesky.533), custom_call_target="Cholesky" | custom-call | tf_op jit(solution)/shard_map/jit(cholesky)/cholesky | solution.py:158
  379.6 10.2 %custom-call.67 = f32[1,128,128]{1,2,0:T(8,128)S(1)} custom-call(f32[1,128,128]{2,1,0:T(8,128)S(1)} %get-tuple-element.420), custom_call_target="InvertDiagBlocksLowerTriangular" | custom-call | tf_op jit(solution)/shard_map/jit(cholesky)/cholesky | solution.py:158
  393.1 11.7 %cholesky.460 = f32[128,128]{1,0:T(8,128)S(1)} custom-call(f32[128,128]{1,0:T(8,128)S(1)} %cholesky.538), custom_call_target="Cholesky" | custom-call | tf_op jit(solution)/shard_map/jit(cholesky)/cholesky | solution.py:158
  406.1 9.8 %custom-call.68 = f32[1,128,128]{1,2,0:T(8,128)S(1)} custom-call(f32[1,128,128]{2,1,0:T(8,128)S(1)} %get-tuple-element.417), custom_call_target="InvertDiagBlocksLowerTriangular" | custom-call | tf_op jit(solution)/shard_map/jit(cholesky)/cholesky | solution.py:158
  418.9 11.9 %cholesky.480 = f32[128,128]{1,0:T(8,128)S(1)} custom-call(f32[128,128]{1,0:T(8,128)S(1)} %cholesky.543), custom_call_target="Cholesky" | custom-call | tf_op jit(solution)/shard_map/jit(cholesky)/cholesky | solution.py:158
  432.1 9.8 %custom-call.69 = f32[1,128,128]{1,2,0:T(8,128)S(1)} custom-call(f32[1,128,128]{2,1,0:T(8,128)S(1)} %get-tuple-element.414), custom_call_target="InvertDiagBlocksLowerTriangular" | custom-call | tf_op jit(solution)/shard_map/jit(cholesky)/cholesky | solution.py:158
  444.5 11.7 %cholesky.498 = f32[128,128]{1,0:T(8,128)S(1)} custom-call(f32[128,128]{1,0:T(8,128)S(1)} %convolution_subtract_fusion.13), custom_call_target="Cholesky" | custom-call | tf_op jit(solution)/shard_map/jit(cholesky)/cholesky | solution.py:158
  462.6 6.6 %fusion.1 = (f32[1024,1024]{1,0:T(8,128)}, f32[1024,1024]{1,0:T(8,128)}) fusion(f32[1024,1024]{1,0:T(8,128)} %get-tuple-element.412, pred[]{:T(512)S(6)} %cholesky.513), kind=kLoop, calls=%fused_computation.7 | loop fusion | flops 4194304 | bytes 12582913 | tf_op jit(solution)/shard_map/jit(_solve_triangular)/triangular_solve | solution.py:159
  469.2 23.2 %while.1 = (s32[]{:T(128)}, f32[1024,1024]{1,0:T(8,128)}, s32[8,2]{0,1:T(2,128)S(1)}, f32[8,128,128]{2,1,0:T(8,128)S(1)}, s32[]{:T(128)}) while((s32[]{:T(128)}, f32[1024,1024]{1,0:T(8,128)}, s32[8,2]{0,1:T(2,128)S(1)}, f32[8,128,128]{2,1,0:T(8,128)S(1)}, s32[]{:T(128)}) %tuple.396), condition=%wide.while_cond, body=%wide.while_body.sunk | while | flops 2 | bytes 131189 | solution.py:159
  492.4 79.4 %custom-call.70 = f32[8,128,128]{1,2,0:T(8,128)} custom-call(f32[8,128,128]{2,1,0:T(8,128)S(1)} %get-tuple-element.10), custom_call_target="InvertDiagBlocksLowerTriangular" | custom-call | tf_op jit(solution)/shard_map/jit(_solve_triangular)/triangular_solve | solution.py:159
  595.5 5.5 all-to-all-start.1
  601.7 17.3 %gather_fusion = f32[1024]{0:T(1024)S(1)} fusion(f32[1024,1024]{1,0:T(8,128)} %get-tuple-element.320, s32[1024]{0:T(1024)S(1)} %bitcast.397), kind=kCustom, calls=%fused_computation | custom fusion | bytes 16384 | tf_op jit(solution)/shard_map/jit(diagonal)/cond/branch_0_fun/gather | solution.py:163
  (326 shorter events, 204.9 us)
Async XLA Ops:
  7.2 234.4 %all-reduce.3.cloned.1.call-start = ((), (), s32[]{:S(2)}) async-start(), calls=%async_computation.2 | async-start | bytes 8388608 | tf_op jit(solution)/shard_map/psum | solution.py:157
  8.1 12.2 %collective-permute-start.1 = (f32[2,2,128]{2,1,0:T(2,128)S(1)}, f32[2,2,128]{2,1,0:T(2,128)S(1)}, u32[]{:S(2)}, u32[]{:S(2)}) collective-permute-start(f32[2,2,128]{2,1,0:T(2,128)S(1)} %pad_maximum_fusion.11), channel_id=1, source_target_pairs={{4,0},{8,4},{12,8},{0,12},{5,1},{9,5},{13,9},{1,13},{6,2},{10,6},{... | collective-permute-start | bytes 6152 | tf_op jit(solution)/shard_map/ppermute | solution.py:22
  12.3 8.1 %collective-permute-start = (f32[2,2,128]{2,1,0:T(2,128)S(1)}, f32[2,2,128]{2,1,0:T(2,128)S(1)}, u32[]{:S(2)}, u32[]{:S(2)}) collective-permute-start(f32[2,2,128]{2,1,0:T(2,128)S(1)} %pad_maximum_fusion.11), channel_id=1, source_target_pairs={{0,4},{4,8},{8,12},{12,0},{1,5},{5,9},{9,13},{13,1},{2,6},{6,10},{... | collective-permute-start | bytes 6152 | tf_op jit(solution)/shard_map/ppermute | solution.py:19
  14.4 28.2 %collective-permute-start.7 = (bf16[2,2,128,256]{3,2,0,1:T(8,128)(2,1)S(1)}, bf16[2,2,128,256]{3,2,0,1:T(8,128)(2,1)S(1)}, u32[]{:S(2)}, u32[]{:S(2)}) collective-permute-start(bf16[2,2,128,256]{3,2,0,1:T(8,128)(2,1)S(1)} %get-tuple-element.327), channel_id=1, source_target_pairs={{4,0},{8,4},{12,8},{0,12},{5,1},{9,5},{13,9},{1,13},{6,2},{10,6},{... | collective-permute-start | bytes 786440 | tf_op jit(solution)/shard_map/ppermute | solution.py:22
  17.7 26.6 %collective-permute-start.6 = (bf16[2,2,128,256]{3,2,0,1:T(8,128)(2,1)S(1)}, bf16[2,2,128,256]{3,2,0,1:T(8,128)(2,1)S(1)}, u32[]{:S(2)}, u32[]{:S(2)}) collective-permute-start(bf16[2,2,128,256]{3,2,0,1:T(8,128)(2,1)S(1)} %get-tuple-element.327), channel_id=1, source_target_pairs={{0,4},{4,8},{8,12},{12,0},{1,5},{5,9},{9,13},{13,1},{2,6},{6,10},{... | collective-permute-start | bytes 786440 | tf_op jit(solution)/shard_map/ppermute | solution.py:19
  18.6 4.9 copy-start.3
  18.6 4.9 copy-start.4
  18.7 4.9 copy-start.2
  23.7 4.2 collective-permute-start.3
  27.0 4.2 collective-permute-start.2
  34.6 2.5 collective-permute-start.5
  35.0 4.2 collective-permute-start.4
  57.1 7.5 %collective-permute-start.9 = (bf16[2,2,128,256]{3,2,0,1:T(8,128)(2,1)S(1)}, bf16[2,2,128,256]{3,2,0,1:T(8,128)(2,1)S(1)}, u32[]{:S(2)}, u32[]{:S(2)}) collective-permute-start(bf16[2,2,128,256]{3,2,0,1:T(8,128)(2,1)S(1)} %get-tuple-element.325), channel_id=1, source_target_pairs={{4,0},{8,4},{12,8},{0,12},{5,1},{9,5},{13,9},{1,13},{6,2},{10,6},{... | collective-permute-start | bytes 786440 | tf_op jit(solution)/shard_map/ppermute | solution.py:22
  58.0 8.5 %collective-permute-start.8 = (bf16[2,2,128,256]{3,2,0,1:T(8,128)(2,1)S(1)}, bf16[2,2,128,256]{3,2,0,1:T(8,128)(2,1)S(1)}, u32[]{:S(2)}, u32[]{:S(2)}) collective-permute-start(bf16[2,2,128,256]{3,2,0,1:T(8,128)(2,1)S(1)} %get-tuple-element.325), channel_id=1, source_target_pairs={{0,4},{4,8},{8,12},{12,0},{1,5},{5,9},{9,13},{13,1},{2,6},{6,10},{... | collective-permute-start | bytes 786440 | tf_op jit(solution)/shard_map/ppermute | solution.py:19
  79.4 5.5 collective-permute-start.11
  80.8 12.8 %collective-permute-start.10 = (bf16[2,2,128,256]{3,2,0,1:T(8,128)(2,1)S(1)}, bf16[2,2,128,256]{3,2,0,1:T(8,128)(2,1)S(1)}, u32[]{:S(2)}, u32[]{:S(2)}) collective-permute-start(bf16[2,2,128,256]{3,2,0,1:T(8,128)(2,1)S(1)} %get-tuple-element.322), channel_id=1, source_target_pairs={{0,4},{4,8},{8,12},{12,0},{1,5},{5,9},{9,13},{13,1},{2,6},{6,10},{... | collective-permute-start | bytes 786440 | tf_op jit(solution)/shard_map/ppermute | solution.py:19
  256.8 1.9 copy-start
  571.8 7.2 %copy-start.1 = (f32[8,128,128]{1,2,0:T(8,128)S(1)}, f32[8,128,128]{1,2,0:T(8,128)}, u32[]{:S(2)}) copy-start(f32[8,128,128]{1,2,0:T(8,128)} %custom-call.70) | copy-start | bytes 1572868
  595.5 24.2 %all-to-all-start.1 = ((f32[4,1,65536]{2,1,0:T(1,128)}), f32[4,1,65536]{2,1,0:T(1,128)S(1)}, u32[]{:S(2)}, u32[]{:S(2)}) async-start(f32[4,1,65536]{2,1,0:T(1,128)} %reshape.847), calls=%async_computation.1 | async-start | bytes 2097152 | tf_op jit(solution)/shard_map/all_to_all | solution.py:160
Sparse Core Ops, SparseCore 0:
  133.6 107.9 all-reduce.2
where the time goes:
time: 647 us; the launch traced here: 640 us
  other arithmetic  287 us (44%)
  waiting for transfers between devices  130 us (20%)
  matrix products  87.6 us (14%)
  local copies, waits for them, and re-layouts  71.5 us (11%)
  starting transfers between devices  21.9 us (3%)
  blocking collectives  21.8 us (3%)
  between operations  20.3 us (3%)
    another operation x31, other arithmetic, body(): factor = jnp.linalg.cholesky(gram * gram_scale)  173 us
    psum x1, waiting for transfers between devices, body(): gram = lax.psum(partial_value, ('space', 'tangent'))  108 us
    another operation x3, other arithmetic, body(): jax.scipy.linalg.solve_triangular(factor, flat_rows.T, lower=True)  86 us
    another operation x14, matrix products, body(): factor = jnp.linalg.cholesky(gram * gram_scale)  23.1 us
    another operation x24, local copies, waits for them, and re-layouts  23 us
    all_to_all x1, blocking collectives, body(): lax.all_to_all(final, 'tangent', split_axis=2, concat_axis=3, tiled=True)  21.8 us
    gather x1, local copies, waits for them, and re-layouts, body(): log_diag = jnp.log(jnp.diagonal(factor))  17.3 us
    another operation x15, matrix products, body(): jax.scipy.linalg.solve_triangular(factor, flat_rows.T, lower=True)  14.7 us
  transfers between devices with their start and end apart: 14, of which 9 were waited for; matrix products, arithmetic and copies ran while one was open for 6% of the time, Pallas kernels for 0%

commit v1 on v0

--- a/solution.py
+++ b/solution.py
@@ -8,6 +8,17 @@
 CUT2 = 2.0 ** (1.0 / 3.0)
 PARK = 1000.0
 HIGH = lax.Precision.HIGHEST
+
+
+def in_blocks(array, dim, size):
+    before, after = (array.shape[:dim], array.shape[dim + 1 :])
+    return jnp.moveaxis(array.reshape(*before, size, -1, *after), dim, 0)
+
+
+def in_order(pieces, dim):
+    pieces = jnp.moveaxis(pieces, 0, dim)
+    lengths = pieces.shape
+    return pieces.reshape(*lengths[:dim], lengths[dim] * lengths[dim + 1], *lengths[dim + 2 :])
 
 
 def padded(block, sides, width):
@@ -157,9 +168,15 @@
     gram = lax.psum(partial_value, ("space", "tangent"))
     factor = jnp.linalg.cholesky(gram * gram_scale)
     solved = jax.scipy.linalg.solve_triangular(factor, flat_rows.T, lower=True).T
-    columns_out = lax.all_to_all(
-        solved.reshape(rows_form.shape), "tangent", split_axis=3, concat_axis=2, tiled=True
-    )
+    x = solved.reshape(rows_form.shape)
+    count_2, index = (lax.axis_size("tangent"), lax.axis_index("tangent"))
+    tiles = in_blocks(x, 3, count_2)
+    done = [tiles[index]]
+    for step in range(1, count_2):
+        sent = tiles[index ^ step]
+        done.append(lax.ppermute(sent, "tangent", [(i_2, i_2 ^ step) for i_2 in range(count_2)]))
+    tiles = jnp.stack(done)[index ^ jnp.arange(count_2)]
+    columns_out = in_order(tiles, 2)
     log_diag = jnp.log(jnp.diagonal(factor))
     stretch = lax.dynamic_slice_in_dim(log_diag, lax.axis_index("tangent") * block_cols, block_cols)
     return (phase, columns_out, stretch)

time: 647 us -> 626 us (0.968)
  local copies, waits for them, and re-layouts: 71.5 us -> 56.5 us
    unnamed x13 -> x15, local copies, waits for them, and re-layouts: 11.7 us -> 2.22 us
    another operation x24 -> x26, local copies, waits for them, and re-layouts: 23 us -> 24.6 us
  transfers between devices with their start and end apart: 14 -> 16, of which waited for: 9 -> 9; matrix products, arithmetic and copies ran while one was open for 6% -> 6% of each run, Pallas kernels for 0% -> 0%
where the time goes in v1:
time: 626 us; the launch traced here: 619 us
  other arithmetic  283 us (45%)
  waiting for transfers between devices  130 us (21%)
  matrix products  87.6 us (14%)
  local copies, waits for them, and re-layouts  56.5 us (9%)
  blocking collectives  21.8 us (3%)
  between operations  20.4 us (3%)
  starting transfers between devices  19.9 us (3%)
    another operation x31, other arithmetic, body(): factor = jnp.linalg.cholesky(gram * gram_scale)  173 us
    psum x1, waiting for transfers between devices, body(): gram = lax.psum(partial_value, ('space', 'tangent'))  108 us
    another operation x3, other arithmetic, body(): jax.scipy.linalg.solve_triangular(factor, flat_rows.T, lower=True)  86 us
    another operation x25, local copies, waits for them, and re-layouts  24.1 us
    another operation x14, matrix products, body(): factor = jnp.linalg.cholesky(gram * gram_scale)  23.1 us
    all_to_all x1, blocking collectives, body(): lax.all_to_all(final, 'tangent', split_axis=2, concat_axis=3, tiled=True)  21.8 us
    gather x1, local copies, waits for them, and re-layouts, body(): log_diag = jnp.log(jnp.diagonal(factor))  16.8 us
    another operation x15, matrix products, body(): jax.scipy.linalg.solve_triangular(factor, flat_rows.T, lower=True)  14.7 us
  transfers between devices with their start and end apart: 16, of which 9 were waited for; matrix products, arithmetic and copies ran while one was open for 6% of the time, Pallas kernels for 0%

profile of v1, /device:TPU:1, one launch (start us, length us, event | category | flops | bytes accessed | tf_op | source)
XLA Modules:
  0.0 619.1 jit_solution(5081487455835537031)
XLA Ops:
  86.5 7.0 %collective-permute-done.10 = bf16[2,2,128,256]{3,2,0,1:T(8,128)(2,1)S(1)} collective-permute-done((bf16[2,2,128,256]{3,2,0,1:T(8,128)(2,1)S(1)}, bf16[2,2,128,256]{3,2,0,1:T(8,128)(2,1)S(1)}, u32[]{:S(2)}, u32[]{:S(2)}) %collective-permute-start.10) | collective-permute-done | bytes 262176 | tf_op jit(solution)/shard_map/ppermute | solution.py:30
  105.6 21.8 %all_to_all.15 = f32[2,4,128,256]{3,0,1,2:T(2,128)S(1)} all-to-all(f32[2,4,128,256]{3,0,1,2:T(2,128)S(1)} %copy.23), channel_id=1, replica_groups=mesh['groups'=2,'space'=4,'tangent'=4] {'tangent'}, dimensions={2} | all-to-all | bytes 2097152 | tf_op jit(solution)/shard_map/all_to_all | solution.py:157
  128.3 5.2 fusion.2421
  133.9 107.5 %all-reduce.3.cloned.1.call-done = f32[1024,1024]{0,1:T(8,128)} async-done(((f32[1024,1024]{0,1:T(8,128)}), f32[1024,1024]{0,1:T(8,128)}) %all-reduce.3.cloned.1.call-update) | async-done | bytes 4194320 | tf_op jit(solution)/shard_map/psum | solution.py:168
  246.5 5.7 copy.26
  258.6 11.7 %cholesky.187 = f32[128,128]{1,0:T(8,128)S(1)} custom-call(f32[128,128]{1,0:T(8,128)S(1)} %cholesky.514), custom_call_target="Cholesky" | custom-call | tf_op jit(solution)/shard_map/jit(cholesky)/cholesky | solution.py:169
  271.0 9.8 %custom-call.63 = f32[1,128,128]{1,2,0:T(8,128)S(1)} custom-call(f32[1,128,128]{2,1,0:T(8,128)S(1)} %get-tuple-element.436), custom_call_target="InvertDiagBlocksLowerTriangular" | custom-call | tf_op jit(solution)/shard_map/jit(cholesky)/cholesky | solution.py:169
  287.2 11.9 %cholesky.209 = f32[128,128]{1,0:T(8,128)S(1)} custom-call(f32[128,128]{1,0:T(8,128)S(1)} %cholesky.518), custom_call_target="Cholesky" | custom-call | tf_op jit(solution)/shard_map/jit(cholesky)/cholesky | solution.py:169
  300.4 9.8 %custom-call.64 = f32[1,128,128]{1,2,0:T(8,128)S(1)} custom-call(f32[1,128,128]{2,1,0:T(8,128)S(1)} %get-tuple-element.433), custom_call_target="InvertDiagBlocksLowerTriangular" | custom-call | tf_op jit(solution)/shard_map/jit(cholesky)/cholesky | solution.py:169
  313.5 11.7 %cholesky.402 = f32[128,128]{1,0:T(8,128)S(1)} custom-call(f32[128,128]{1,0:T(8,128)S(1)} %cholesky.523), custom_call_target="Cholesky" | custom-call | tf_op jit(solution)/shard_map/jit(cholesky)/cholesky | solution.py:169
  326.6 9.8 %custom-call.65 = f32[1,128,128]{1,2,0:T(8,128)S(1)} custom-call(f32[1,128,128]{2,1,0:T(8,128)S(1)} %get-tuple-element.430), custom_call_target="InvertDiagBlocksLowerTriangular" | custom-call | tf_op jit(solution)/shard_map/jit(cholesky)/cholesky | solution.py:169
  339.9 11.9 %cholesky.421 = f32[128,128]{1,0:T(8,128)S(1)} custom-call(f32[128,128]{1,0:T(8,128)S(1)} %cholesky.528), custom_call_target="Cholesky" | custom-call | tf_op jit(solution)/shard_map/jit(cholesky)/cholesky | solution.py:169
  353.2 9.8 %custom-call.66 = f32[1,128,128]{1,2,0:T(8,128)S(1)} custom-call(f32[1,128,128]{2,1,0:T(8,128)S(1)} %get-tuple-element.427), custom_call_target="InvertDiagBlocksLowerTriangular" | custom-call | tf_op jit(solution)/shard_map/jit(cholesky)/cholesky | solution.py:169
  366.4 11.7 %cholesky.440 = f32[128,128]{1,0:T(8,128)S(1)} custom-call(f32[128,128]{1,0:T(8,128)S(1)} %cholesky.533), custom_call_target="Cholesky" | custom-call | tf_op jit(solution)/shard_map/jit(cholesky)/cholesky | solution.py:169
  379.5 10.2 %custom-call.67 = f32[1,128,128]{1,2,0:T(8,128)S(1)} custom-call(f32[1,128,128]{2,1,0:T(8,128)S(1)} %get-tuple-element.424), custom_call_target="InvertDiagBlocksLowerTriangular" | custom-call | tf_op jit(solution)/shard_map/jit(cholesky)/cholesky | solution.py:169
  393.1 11.7 %cholesky.460 = f32[128,128]{1,0:T(8,128)S(1)} custom-call(f32[128,128]{1,0:T(8,128)S(1)} %cholesky.538), custom_call_target="Cholesky" | custom-call | tf_op jit(solution)/shard_map/jit(cholesky)/cholesky | solution.py:169
  406.0 9.8 %custom-call.68 = f32[1,128,128]{1,2,0:T(8,128)S(1)} custom-call(f32[1,128,128]{2,1,0:T(8,128)S(1)} %get-tuple-element.421), custom_call_target="InvertDiagBlocksLowerTriangular" | custom-call | tf_op jit(solution)/shard_map/jit(cholesky)/cholesky | solution.py:169
  418.9 11.9 %cholesky.480 = f32[128,128]{1,0:T(8,128)S(1)} custom-call(f32[128,128]{1,0:T(8,128)S(1)} %cholesky.543), custom_call_target="Cholesky" | custom-call | tf_op jit(solution)/shard_map/jit(cholesky)/cholesky | solution.py:169
  432.0 9.8 %custom-call.69 = f32[1,128,128]{1,2,0:T(8,128)S(1)} custom-call(f32[1,128,128]{2,1,0:T(8,128)S(1)} %get-tuple-element.418), custom_call_target="InvertDiagBlocksLowerTriangular" | custom-call | tf_op jit(solution)/shard_map/jit(cholesky)/cholesky | solution.py:169
  444.4 11.7 %cholesky.498 = f32[128,128]{1,0:T(8,128)S(1)} custom-call(f32[128,128]{1,0:T(8,128)S(1)} %convolution_subtract_fusion.13), custom_call_target="Cholesky" | custom-call | tf_op jit(solution)/shard_map/jit(cholesky)/cholesky | solution.py:169
  462.5 6.6 %fusion.1 = (f32[1024,1024]{1,0:T(8,128)}, f32[1024,1024]{1,0:T(8,128)}) fusion(f32[1024,1024]{1,0:T(8,128)} %get-tuple-element.416, pred[]{:T(512)S(6)} %cholesky.513), kind=kLoop, calls=%fused_computation.8 | loop fusion | flops 4194304 | bytes 12582913 | tf_op jit(solution)/shard_map/jit(_solve_triangular)/triangular_solve | solution.py:170
  469.1 23.2 %while.1 = (s32[]{:T(128)}, f32[1024,1024]{1,0:T(8,128)}, s32[8,2]{0,1:T(2,128)S(1)}, f32[8,128,128]{2,1,0:T(8,128)S(1)}, s32[]{:T(128)}) while((s32[]{:T(128)}, f32[1024,1024]{1,0:T(8,128)}, s32[8,2]{0,1:T(2,128)S(1)}, f32[8,128,128]{2,1,0:T(8,128)S(1)}, s32[]{:T(128)}) %tuple.399), condition=%wide.while_cond, body=%wide.while_body.sunk | while | flops 2 | bytes 131189 | solution.py:170
  492.3 79.4 %custom-call.70 = f32[8,128,128]{1,2,0:T(8,128)} custom-call(f32[8,128,128]{2,1,0:T(8,128)S(1)} %get-tuple-element.10), custom_call_target="InvertDiagBlocksLowerTriangular" | custom-call | tf_op jit(solution)/shard_map/jit(_solve_triangular)/triangular_solve | solution.py:170
  592.7 16.8 %gather_fusion.1 = f32[1024]{0:T(1024)S(1)} fusion(f32[1024,1024]{1,0:T(8,128)} %get-tuple-element.320, s32[1024]{0:T(1024)S(1)} %bitcast.409), kind=kCustom, calls=%fused_computation.1 | custom fusion | bytes 16384 | tf_op jit(solution)/shard_map/jit(diagonal)/cond/branch_0_fun/gather | solution.py:180
  (335 shorter events, 185.2 us)
Async XLA Ops:
  7.2 234.3 %all-reduce.3.cloned.1.call-start = ((), (), s32[]{:S(2)}) async-start(), calls=%async_computation.1 | async-start | bytes 8388608 | tf_op jit(solution)/shard_map/psum | solution.py:168
  8.1 12.2 %collective-permute-start.1 = (f32[2,2,128]{2,1,0:T(2,128)S(1)}, f32[2,2,128]{2,1,0:T(2,128)S(1)}, u32[]{:S(2)}, u32[]{:S(2)}) collective-permute-start(f32[2,2,128]{2,1,0:T(2,128)S(1)} %pad_maximum_fusion.12), channel_id=1, source_target_pairs={{4,0},{8,4},{12,8},{0,12},{5,1},{9,5},{13,9},{1,13},{6,2},{10,6},{... | collective-permute-start | bytes 6152 | tf_op jit(solution)/shard_map/ppermute | solution.py:33
  12.3 8.1 %collective-permute-start = (f32[2,2,128]{2,1,0:T(2,128)S(1)}, f32[2,2,128]{2,1,0:T(2,128)S(1)}, u32[]{:S(2)}, u32[]{:S(2)}) collective-permute-start(f32[2,2,128]{2,1,0:T(2,128)S(1)} %pad_maximum_fusion.12), channel_id=1, source_target_pairs={{0,4},{4,8},{8,12},{12,0},{1,5},{5,9},{9,13},{13,1},{2,6},{6,10},{... | collective-permute-start | bytes 6152 | tf_op jit(solution)/shard_map/ppermute | solution.py:30
  14.4 28.2 %collective-permute-start.7 = (bf16[2,2,128,256]{3,2,0,1:T(8,128)(2,1)S(1)}, bf16[2,2,128,256]{3,2,0,1:T(8,128)(2,1)S(1)}, u32[]{:S(2)}, u32[]{:S(2)}) collective-permute-start(bf16[2,2,128,256]{3,2,0,1:T(8,128)(2,1)S(1)} %get-tuple-element.327), channel_id=1, source_target_pairs={{4,0},{8,4},{12,8},{0,12},{5,1},{9,5},{13,9},{1,13},{6,2},{10,6},{... | collective-permute-start | bytes 786440 | tf_op jit(solution)/shard_map/ppermute | solution.py:33
  17.7 26.6 %collective-permute-start.6 = (bf16[2,2,128,256]{3,2,0,1:T(8,128)(2,1)S(1)}, bf16[2,2,128,256]{3,2,0,1:T(8,128)(2,1)S(1)}, u32[]{:S(2)}, u32[]{:S(2)}) collective-permute-start(bf16[2,2,128,256]{3,2,0,1:T(8,128)(2,1)S(1)} %get-tuple-element.327), channel_id=1, source_target_pairs={{0,4},{4,8},{8,12},{12,0},{1,5},{5,9},{9,13},{13,1},{2,6},{6,10},{... | collective-permute-start | bytes 786440 | tf_op jit(solution)/shard_map/ppermute | solution.py:30
  18.6 4.9 copy-start.3
  18.6 4.9 copy-start.4
  18.7 4.9 copy-start.2
  23.7 4.2 collective-permute-start.3
  27.0 4.2 collective-permute-start.2
  34.6 2.5 collective-permute-start.5
  35.0 4.2 collective-permute-start.4
  57.1 7.5 %collective-permute-start.9 = (bf16[2,2,128,256]{3,2,0,1:T(8,128)(2,1)S(1)}, bf16[2,2,128,256]{3,2,0,1:T(8,128)(2,1)S(1)}, u32[]{:S(2)}, u32[]{:S(2)}) collective-permute-start(bf16[2,2,128,256]{3,2,0,1:T(8,128)(2,1)S(1)} %get-tuple-element.325), channel_id=1, source_target_pairs={{4,0},{8,4},{12,8},{0,12},{5,1},{9,5},{13,9},{1,13},{6,2},{10,6},{... | collective-permute-start | bytes 786440 | tf_op jit(solution)/shard_map/ppermute | solution.py:33
  58.0 8.5 %collective-permute-start.8 = (bf16[2,2,128,256]{3,2,0,1:T(8,128)(2,1)S(1)}, bf16[2,2,128,256]{3,2,0,1:T(8,128)(2,1)S(1)}, u32[]{:S(2)}, u32[]{:S(2)}) collective-permute-start(bf16[2,2,128,256]{3,2,0,1:T(8,128)(2,1)S(1)} %get-tuple-element.325), channel_id=1, source_target_pairs={{0,4},{4,8},{8,12},{12,0},{1,5},{5,9},{9,13},{13,1},{2,6},{6,10},{... | collective-permute-start | bytes 786440 | tf_op jit(solution)/shard_map/ppermute | solution.py:30
  79.4 5.5 collective-permute-start.11
  80.8 12.7 %collective-permute-start.10 = (bf16[2,2,128,256]{3,2,0,1:T(8,128)(2,1)S(1)}, bf16[2,2,128,256]{3,2,0,1:T(8,128)(2,1)S(1)}, u32[]{:S(2)}, u32[]{:S(2)}) collective-permute-start(bf16[2,2,128,256]{3,2,0,1:T(8,128)(2,1)S(1)} %get-tuple-element.322), channel_id=1, source_target_pairs={{0,4},{4,8},{8,12},{12,0},{1,5},{5,9},{9,13},{13,1},{2,6},{6,10},{... | collective-permute-start | bytes 786440 | tf_op jit(solution)/shard_map/ppermute | solution.py:30
  256.7 1.9 copy-start
  571.7 7.2 %copy-start.1 = (f32[8,128,128]{1,2,0:T(8,128)S(1)}, f32[8,128,128]{1,2,0:T(8,128)}, u32[]{:S(2)}) copy-start(f32[8,128,128]{1,2,0:T(8,128)} %custom-call.70) | copy-start | bytes 1572868
  588.5 21.7 %collective-permute-start.12 = (f32[2,4,32,256]{3,2,1,0:T(8,128)S(1)}, f32[2,4,32,256]{3,2,1,0:T(8,128)S(1)}, u32[]{:S(2)}, u32[]{:S(2)}) collective-permute-start(f32[2,4,32,256]{3,2,1,0:T(8,128)S(1)} %bitcast.428), channel_id=1, source_target_pairs={{0,1},{1,0},{2,3},{3,2},{4,5},{5,4},{6,7},{7,6},{8,9},{9,8},{10,11... | collective-permute-start | bytes 786440 | tf_op jit(solution)/shard_map/ppermute | solution.py:177
  590.4 19.8 %collective-permute-start.13 = (f32[2,4,32,256]{3,2,1,0:T(8,128)S(1)}, f32[2,4,32,256]{3,2,1,0:T(8,128)S(1)}, u32[]{:S(2)}, u32[]{:S(2)}) collective-permute-start(f32[2,4,32,256]{3,2,1,0:T(8,128)S(1)} %bitcast.427), channel_id=1, source_target_pairs={{0,2},{1,3},{2,0},{3,1},{4,6},{5,7},{6,4},{7,5},{8,10},{9,11},{10,... | collective-permute-start | bytes 786440 | tf_op jit(solution)/shard_map/ppermute | solution.py:177
  591.2 19.0 %collective-permute-start.14 = (f32[2,4,32,256]{3,2,1,0:T(8,128)S(1)}, f32[2,4,32,256]{3,2,1,0:T(8,128)S(1)}, u32[]{:S(2)}, u32[]{:S(2)}) collective-permute-start(f32[2,4,32,256]{3,2,1,0:T(8,128)S(1)} %bitcast.426), channel_id=1, source_target_pairs={{0,3},{1,2},{2,1},{3,0},{4,7},{5,6},{6,5},{7,4},{8,11},{9,10},{10,... | collective-permute-start | bytes 786440 | tf_op jit(solution)/shard_map/ppermute | solution.py:177
Sparse Core Ops, SparseCore 0:
  133.6 107.8 all-reduce.2
